TPU v7x, 1024 devices: a whole 4x4x32 slice. The times are simulated.
1024 devices in a mesh: row: 16 (over z_lo, core), col: 64 (over z_hi, x, y).
Axes of the slice: x: 4, y: 4, z: 32 (z_hi: 4, z_lo: 8; z = z_hi * 8 + z_lo), core: 2. Of those that a mesh axis runs over, the one named last changes fastest.
Arguments:
- features: bfloat16 [32768, 512], P(('row', 'col')), may hold values from -6 to 6
- self_weight: bfloat16 [512, 512], replicated, may hold values from -0.25 to 0.25
- neigh_weight: bfloat16 [512, 512], replicated, may hold values from -0.25 to 0.25
- tiles: bfloat16 [16, 2048, 128, 128], P('row', 'col'), may hold values from 0 to 1, as said below
- tile_pos: int32 [16, 2048], P('row', 'col'), may hold values from 0 to 63, as said below
- tile_count: int32 [16, 64], P('row', 'col'), may hold values from 1 to 32, as said below
- degree: int32 [32768], P(('row', 'col')), may hold values from 256 to 2047
- cotangent: bfloat16 [32768, 512], P(('row', 'col')), may hold values from -0.029907227 to 0.029907227
Outputs:
- hidden: bfloat16 [32768, 512], P(('row', 'col'))
- self_weight_gradient: float32 [512, 512], replicated
- grad_neigh: float32 [512, 512], replicated
Inputs may be any that keep to these rules, and one draw needn't show every extreme that they name: `tile_pos`: within each block's 32 slots the positions are distinct. `tile_count`: some block is full in every draw. `tiles`: entries are zero or between 0.25 and 1.
All inputs are finite; a program needn't handle non-finite values.
Results may differ from a plain program's by a relative error of at most 0.0055.
Values may be sent and summed in bfloat16 or wider, within the bound.
A program may use at most 32 MiB of HBM per device.

v0:
```python
import jax
import jax.numpy as jnp
from jax import lax
from jax.sharding import PartitionSpec as P


def add_tiles(
    running, tile_values_array, positions, live_count, feature_panel, tile_extent, tile_cols
):
    slot_total = tile_values_array.shape[0]
    group_size = 4

    def one_group(group_index, totals):
        for offset in range(group_size):
            tile_slot = jnp.minimum(group_index * group_size + offset, slot_total - 1)
            position = lax.dynamic_index_in_dim(positions, tile_slot, 0, keepdims=False)
            tile_value = lax.dynamic_index_in_dim(tile_values_array, tile_slot, 0, keepdims=False)
            is_live = group_index * group_size + offset < live_count
            tile_value = jnp.where(is_live, tile_value, jnp.zeros_like(tile_value))
            columns = lax.dynamic_slice_in_dim(
                feature_panel, position % tile_cols * tile_extent, tile_extent, 0
            )
            starting = position // tile_cols * tile_extent
            current = lax.dynamic_slice_in_dim(totals, starting, tile_extent, 0)
            product = jnp.dot(tile_value, columns, preferred_element_type=jnp.float32)
            totals = lax.dynamic_update_slice_in_dim(totals, current + product, starting, 0)
        return totals

    return lax.fori_loop(0, (live_count + group_size - 1) // group_size, one_group, running)


def per_device(features, self_weight, neigh_weight, tiles, tile_pos, tile_count, degree, cotangent):
    tile_extent = tiles.shape[2]
    feature_panel = lax.all_gather(features, "row", axis=0, tiled=True)
    tile_cols = feature_panel.shape[0] // tile_extent
    block_rows = features.shape[0] * lax.axis_size("col")
    tile_values_array = tiles[0]
    positions = tile_pos[0]
    own_count = tile_count[0, 0]
    empty = jnp.zeros((block_rows, features.shape[1]), jnp.float32)
    partial_sums = add_tiles(
        empty, tile_values_array, positions, own_count, feature_panel, tile_extent, tile_cols
    )
    sums = lax.psum_scatter(partial_sums, "col", scatter_dimension=0, tiled=True)
    scale = lax.rsqrt(degree.astype(jnp.float32))
    aggregated = (sums * scale[:, None]).astype(jnp.bfloat16)
    before = jnp.dot(features, self_weight, preferred_element_type=jnp.float32) + jnp.dot(
        aggregated, neigh_weight, preferred_element_type=jnp.float32
    )
    sigma = jax.nn.sigmoid(before)
    hidden = (before * sigma).astype(jnp.bfloat16)
    gated = (cotangent.astype(jnp.float32) * sigma * (1.0 + before * (1.0 - sigma))).astype(
        jnp.bfloat16
    )
    contract_rows = (((0,), (0,)), ((), ()))
    local_self = lax.dot_general(features, gated, contract_rows, preferred_element_type=jnp.float32)
    local_neigh = lax.dot_general(
        aggregated, gated, contract_rows, preferred_element_type=jnp.float32
    )
    self_weight_gradient, grad_neigh = lax.psum((local_self, local_neigh), ("row", "col"))
    return (hidden, self_weight_gradient, grad_neigh)


def solution(mesh):
    in_specs = (
        P(("row", "col"), None),
        P(),
        P(),
        P("row", "col", None, None),
        P("row", "col"),
        P("row", "col"),
        P(("row", "col")),
        P(("row", "col"), None),
    )
    out_specs = (P(("row", "col"), None), P(), P())
    return jax.shard_map(
        per_device, mesh=mesh, in_specs=in_specs, out_specs=out_specs, check_vma=False
    )
```

profile of v0, /device:TPU:1, one launch (start us, length us, event | category | flops | bytes accessed | tf_op | source)
XLA Modules:
  0.0 1766.4 jit_solution(5073331623042615166)
XLA Ops:
  7.2 0.0 copy-start
  7.2 0.0 copy-start.3
  7.2 0.0 reduce-scatter.2.cloned.1.call-start
  7.9 42.3 %all_gather.3 = bf16[512,512]{1,0:T(8,128)(2,1)S(1)} all-gather(bf16[32,512]{1,0:T(8,128)(2,1)} %param.10), channel_id=1, replica_groups=mesh['row'=16,'col'=64] {'row'}, dimensions={0}, use_global_device_ids=true | all-gather | bytes 557056 | tf_op jit(solution)/shard_map/all_gather | solution.py:34
  50.3 2.5 broadcast_in_dim.4
  52.8 0.0 copy-done.3
  52.8 42.4 %while.13 = (s32[]{:T(128)}, f32[2048,512]{1,0:T(8,128)}, s32[]{:T(128)}, s32[32]{0:T(128)S(1)}, s32[]{:T(128)}, /*index=5*/bf16[32,128,128]{2,1,0:T(8,128)(2,1)...) while((s32[]{:T(128)}, f32[2048,512]{1,0:T(8,128)}, ...), condition=%wide.region_1.2_spmd, body=%wide.region_0.1_spmd.sunk | while | flops 67436592 | bytes 2754161 | solution.py:29
  52.8 0.7 fusion.64
  56.8 1.9 fusion.65
  62.2 1.8 fusion.66
  67.0 1.9 fusion.67
  72.1 1.8 fusion.68
  74.0 0.7 fusion.64
  78.0 1.9 fusion.65
  83.3 1.9 fusion.66
  88.2 1.9 fusion.67
  93.3 1.9 fusion.68
  95.1 0.0 copy-start.5
  95.1 0.0 copy-start.1
  95.1 0.0 copy-start.2
  95.2 0.0 copy-start.4
  95.2 0.0 reduce-scatter.2.cloned.1.call-update
  95.2 0.0 all-reduce.3.cloned.1.call-start
  95.2 0.6 copy-done.5
  95.8 0.4 copy-done.1
  96.2 0.0 copy-done.2
  96.2 0.2 fusion.38
  96.4 720.4 %reduce-scatter.2.cloned.1.call-done = f32[32,512]{1,0:T(8,128)} async-done(((f32[2048,512]{1,0:T(8,128)}), f32[32,512]{1,0:T(8,128)}) %reduce-scatter.2.cloned.1.call-update) | async-done | bytes 65552 | tf_op jit(solution)/shard_map/reduce_scatter | solution.py:44
  816.8 0.0 copy-done
  816.8 1.7 multiply_convert_fusion.1
  818.5 0.0 copy-done.4
  818.6 1.3 convolution_bitcast_fusion
  819.9 2.2 fusion.36
  822.1 0.0 all-reduce.3.cloned.1.call-update
  822.1 932.7 %all-reduce.3.cloned.1.call-done = (f32[512,512]{0,1:T(8,128)}, f32[512,512]{1,0:T(8,128)}) async-done(((f32[512,512]{0,1:T(8,128)}, f32[512,512]{1,0:T(8,128)}), (f32[512,512]{0,1:T(8,128)}, f32[512,512]{1,0:T(8,128)})) %all-reduce.3.cloned.1.call-update) | async-done | bytes 2097168 | tf_op jit(solution)/shard_map/psum | solution.py:60
  1754.8 2.5 copy.11
  1757.3 2.3 copy.25
  (1 shorter events, 0.0 us)
Async XLA Ops:
  7.2 809.7 %copy-start = (bf16[512,512]{1,0:T(8,128)(2,1)S(1)}, bf16[512,512]{1,0:T(8,128)(2,1)}, u32[]{:S(2)}) copy-start(bf16[512,512]{1,0:T(8,128)(2,1)} %param.12) | copy-start | bytes 1572868
  7.2 45.6 %copy-start.3 = (s32[1,32]{1,0:T(1,128)S(1)}, s32[1,32]{1,0:T(1,128)}, u32[]{:S(2)}) copy-start(s32[1,32]{1,0:T(1,128)} %param.14) | copy-start | bytes 388
  7.2 809.6 %reduce-scatter.2.cloned.1.call-start = ((), (), s32[]{:S(2)}) async-start(), calls=%async_computation.1 | async-start | bytes 4259840 | tf_op jit(solution)/shard_map/reduce_scatter | solution.py:44
  95.1 0.7 copy-start.5
  95.1 1.1 copy-start.1
  95.1 1.1 copy-start.2
  95.2 723.4 %copy-start.4 = (bf16[32,512]{1,0:T(8,128)(2,1)S(1)}, bf16[32,512]{1,0:T(8,128)(2,1)}, u32[]{:S(2)}) copy-start(bf16[32,512]{1,0:T(8,128)(2,1)} %param.17) | copy-start | bytes 98308
  95.2 1659.6 %all-reduce.3.cloned.1.call-start = ((), (), s32[]{:S(2)}) async-start(), calls=%async_computation.2 | async-start | bytes 4194304 | tf_op jit(solution)/shard_map/psum | solution.py:60
Sparse Core Ops, SparseCore 0:
  95.3 721.4 reduce-scatter.1
  823.8 930.9 all-reduce.2
where the time goes:
time: 1770 us
  waiting for transfers between devices  1650 us (93%)
  blocking collectives  42.3 us (2%)
  loops' own time  26.2 us (1%)
  matrix products  20.2 us (1%)
    psum x1, waiting for transfers between devices, per_device(): lax.psum((local_self, local_neigh), ('row', 'col'))  933 us
    reduce_scatter x1, waiting for transfers between devices, per_device(): lax.psum_scatter(partial_sums, 'col', scatter_dimension=0, tiled=True)  720 us
    all_gather x1, blocking collectives, per_device(): feature_panel = lax.all_gather(features, 'row', axis=0, tiled=True)  42.3 us
  transfers between devices with their start and end apart: 2, of which 2 were waited for; matrix products, arithmetic and copies ran while one was open for 0% of the time, Pallas kernels for 0%

commit v1 on v0

v1 whole, which is shorter than its diff:
```python
import jax
import jax.numpy as jnp
from jax import lax
from jax.experimental import pallas as pl
from jax.experimental.pallas import tpu as pltpu
from jax.sharding import PartitionSpec as P

MESH = pl.DeviceIdType.MESH
BF16, F32 = jnp.bfloat16, jnp.float32
WIDTH, TILE, ND = 512, 128, 32
HALF = WIDTH // 2


def flip(value, mask, bits):
    out = 0
    for k in range(bits):
        bit = lax.rem(lax.div(value, 1 << k), 2)
        out = out + (1 << k) * ((1 - bit) if (mask >> k) & 1 else bit)
    return out


def mix(value, other, bits):
    out = 0
    for k in range(bits):
        a = lax.rem(lax.div(value, 1 << k), 2)
        b = lax.rem(lax.div(other, 1 << k), 2)
        out = out + (1 << k) * (a + b - 2 * a * b)
    return out


def rows_at(index, count):
    return pl.ds(pl.multiple_of(index * count, count), count)


def kernel(
    features_ref, self_weight_ref, neigh_weight_ref, tiles_ref, slots_ref, degree_ref, cotangent_ref,
    hidden_ref, grads_ref,
    tiles_v, self_v, neigh_v, dense, panel, part0, part1, in_a0, in_a1, mid0, mid1, in_b0, in_b1,
    block, in_c, other, left, gated, left_in, gated_in, section, in_z, groups, final,
    load_sem, ag_s, ag_r, agc_s, agc_r, a_s, a_r, b_s, b_r, c_s, c_r, f_s, f_r, l_s, l_r, g_s, g_r,
    z_s, z_r, zs_s, zs_r, za_s, za_r, xy_s, xy_r, xc_s, xc_r,
):
    row, col = lax.axis_index("row"), lax.axis_index("col")
    core, z_lo = lax.rem(row, 2), lax.div(row, 2)
    z = lax.div(col, 16) * 8 + z_lo
    x, y = lax.rem(lax.div(col, 4), 4), lax.rem(col, 4)
    z_in, z_group = lax.rem(z, 4), lax.div(z, 4)

    def peer(dz=0, dx=0, dy=0, dc=0):
        zp, xp, yp, cp = flip(z, dz, 5), flip(x, dx, 2), flip(y, dy, 2), flip(core, dc, 1)
        return (lax.rem(zp, 8) * 2 + cp, lax.div(zp, 8) * 16 + xp * 4 + yp)

    def send(src, dst, ssem, rsem, to):
        copy = pltpu.make_async_remote_copy(
            src_ref=src, dst_ref=dst, send_sem=ssem, recv_sem=rsem, device_id=to, device_id_type=MESH
        )
        copy.start()
        sent.append(copy)
        return copy

    sent = []
    loads = [
        pltpu.make_async_copy(tiles_ref, tiles_v, load_sem.at[0]),
        pltpu.make_async_copy(self_weight_ref, self_v, load_sem.at[1]),
        pltpu.make_async_copy(neigh_weight_ref, neigh_v, load_sem.at[2]),
    ]
    for load in loads:
        load.start()

    partner = peer(dc=1)
    plane = [(m // 4, m % 4) for m in range(1, 16)]
    peers = [partner]
    peers += [peer(dz=m) for m in range(1, 8)]
    peers += [peer(dz=m) for m in (8, 12, 16, 20, 24, 28)]
    peers += [peer(dx=dx, dy=dy) for dx, dy in plane]
    barrier = pltpu.get_barrier_semaphore()
    for device in peers:
        pl.semaphore_signal(barrier, inc=1, device_id=device, device_id_type=MESH)

    panel[rows_at(row, ND), :] = features_ref[...]
    loads[0].wait()

    def place(t, carry):
        dz = mix(lax.div(t, 4), lax.div(col, 16), 2)
        dx = mix(lax.rem(t, 4), x, 2)
        for q in range(4):
            slot = slots_ref[t * 4 + q]
            tile = tiles_v[jnp.maximum(slot, 0)]
            tile = jnp.where(slot >= 0, tile, jnp.zeros_like(tile))
            for yc in range(4):
                dy = mix(jnp.int32(yc), y, 2)
                dense[dx * 4 + dy, rows_at(dz, ND), q * TILE : (q + 1) * TILE] = tile[yc * ND : (yc + 1) * ND]
        return carry

    lax.fori_loop(0, 16, place, 0)
    pl.semaphore_wait(barrier, len(peers))

    mine = rows_at(row, ND)
    gather = [
        send(features_ref, panel.at[mine, :], ag_s.at[m], ag_r.at[m], peer(dz=m)) for m in range(7, 0, -1)
    ][::-1]
    across = [send(features_ref, panel.at[mine, :], agc_s.at[0], agc_r.at[0], partner)]
    loads[1].wait()
    own_part = jnp.dot(features_ref[...], self_v[...], preferred_element_type=F32)
    for m in range(1, 8):
        gather[m - 1].wait_recv()
        theirs = panel.at[rows_at(flip(z_lo, m, 3) * 2 + core, ND), :]
        across.append(send(theirs, theirs, agc_s.at[m], agc_r.at[m], partner))
    for copy in across:
        copy.wait_recv()

    first, second = [], []
    for dx in (2, 1, 3, 0):
        for part in range(2):
            lhs = dense[dx * 4 + part * 2 : dx * 4 + part * 2 + 2].reshape(2 * TILE, WIDTH)
            product = jnp.dot(lhs, panel[...], preferred_element_type=F32).astype(BF16)
            for k in range(2):
                dy = part * 2 + k
                part0[dx, dy] = product[k * TILE : (k + 1) * TILE, :HALF]
                part1[dy, dx] = product[k * TILE : (k + 1) * TILE, HALF:]
        if dx:
            first.append(send(part0.at[dx], in_a0.at[dx], a_s.at[dx], a_r.at[dx], peer(dx=dx)))
    for dy in (2, 1, 3):
        second.append(send(part1.at[dy], in_a1.at[dy], a_s.at[4 + dy], a_r.at[4 + dy], peer(dy=dy)))

    def total(own, parts):
        out = own.astype(F32)
        for value in parts:
            out = out + value.astype(F32)
        return out

    for copy in first:
        copy.wait_recv()
    first = []
    for k in (2, 1, 3, 0):
        mid0[k] = total(part0[0, k], [in_a0[m, k] for m in (1, 2, 3)]).astype(BF16)
        if k:
            first.append(send(mid0.at[k], in_b0.at[k], b_s.at[k], b_r.at[k], peer(dy=k)))
    for copy in second:
        copy.wait_recv()
    second = []
    for k in (2, 1, 3, 0):
        mid1[k] = total(part1[0, k], [in_a1[m, k] for m in (1, 2, 3)]).astype(BF16)
        if k:
            second.append(send(mid1.at[k], in_b1.at[k], b_s.at[4 + k], b_r.at[4 + k], peer(dx=k)))
    for copy in first:
        copy.wait_recv()
    low = total(mid0[0], [in_b0[m] for m in (1, 2, 3)]).astype(BF16)
    for k in range(4):
        block[k, :, :HALF] = low[k * ND : (k + 1) * ND]
    for copy in second:
        copy.wait_recv()
    high = total(mid1[0], [in_b1[m] for m in (1, 2, 3)]).astype(BF16)
    for k in range(4):
        block[k, :, HALF:] = high[k * ND : (k + 1) * ND]
    far = [send(block.at[k], in_c.at[k], c_s.at[k], c_r.at[k], peer(dz=8 * k)) for k in (2, 1, 3)]
    loads[2].wait()
    degree = jnp.broadcast_to(degree_ref[...].astype(F32), (ND, ND))
    eye = lax.broadcasted_iota(jnp.int32, (ND, ND), 0) == lax.broadcasted_iota(jnp.int32, (ND, ND), 1)
    scale = lax.rsqrt(jnp.sum(jnp.where(eye, degree, 0.0), axis=1, keepdims=True))
    for copy in far:
        copy.wait_recv()
    sums = total(block[0], [in_c[k] for k in (1, 2, 3)])

    aggregated = (sums * scale).astype(BF16)
    before = own_part + jnp.dot(aggregated, neigh_v[...], preferred_element_type=F32)
    sigma = 1.0 / (1.0 + jnp.exp(-before))
    gate = (cotangent_ref[...].astype(F32) * sigma * (1.0 + before * (1.0 - sigma))).astype(BF16)
    hidden_ref[...] = (before * sigma).astype(BF16)
    other[0] = features_ref[...]
    other[1] = aggregated
    gated[0] = gate

    pair = [
        send(gated.at[0], gated.at[1], f_s.at[0], f_r.at[0], partner),
        send(other.at[1 - core], left.at[1], f_s.at[1], f_r.at[1], partner),
    ]
    left[0] = other[core]
    for copy in pair:
        copy.wait_recv()
    swaps = []
    for dx, dy in plane:
        m = dx * 4 + dy
        lanes_x = rows_at(flip(x, dx, 2), TILE)
        lanes_y = rows_at(flip(y, dy, 2), TILE)
        to = peer(dx=dx, dy=dy)
        swaps.append(send(left.at[:, :, lanes_x], left_in.at[m], l_s.at[m], l_r.at[m], to))
        swaps.append(send(gated.at[:, :, lanes_y], gated_in.at[m], g_s.at[m], g_r.at[m], to))
    left_in[0] = left[:, :, rows_at(x, TILE)]
    gated_in[0] = gated[:, :, rows_at(y, TILE)]
    for copy in swaps:
        copy.wait_recv()
    section[...] = lax.dot_general(
        left_in[...].reshape(16 * 2 * ND, TILE),
        gated_in[...].reshape(16 * 2 * ND, TILE),
        (((0,), (0,)), ((), ())),
        preferred_element_type=F32,
    ).reshape(4, ND, TILE)

    near = [
        send(section.at[flip(z_in, m, 2)], in_z.at[m], z_s.at[m], z_r.at[m], peer(dz=m)) for m in (2, 1, 3)
    ]
    for copy in near:
        copy.wait_recv()
    groups[z_group] = (section[z_in] + in_z[1] + in_z[2] + in_z[3]).astype(BF16)
    spread = [
        send(groups.at[z_group], groups.at[z_group], zs_s.at[m], zs_r.at[m], peer(dz=4 * m))
        for m in (4, 3, 5, 2, 6, 1, 7)
    ]
    for copy in spread:
        copy.wait_recv()
    final[rows_at(z_in, ND), :] = total(groups[0], [groups[k] for k in range(1, 8)]).astype(BF16)
    own_rows = final.at[rows_at(z_in, ND), :]
    back = [send(own_rows, own_rows, za_s.at[m], za_r.at[m], peer(dz=m)) for m in (2, 1, 3)]
    for copy in back:
        copy.wait_recv()

    here = grads_ref.at[core, x, :, rows_at(y, TILE)]
    out = [send(final, here, xy_s.at[dx * 4 + dy], xy_r.at[dx * 4 + dy], peer(dx=dx, dy=dy)) for dx, dy in plane]
    last = [send(final, here, xc_s.at[0], xc_r.at[0], partner)]
    grads_ref[core, x, :, rows_at(y, TILE)] = final[...]
    for (dx, dy), copy in zip(plane, out):
        copy.wait_recv()
        there = grads_ref.at[core, flip(x, dx, 2), :, rows_at(flip(y, dy, 2), TILE)]
        m = dx * 4 + dy
        last.append(send(there, there, xc_s.at[m], xc_r.at[m], partner))
    for copy in last:
        copy.wait_recv()
    for copy in sent:
        copy.wait_send()


def per_device(features, self_weight, neigh_weight, tiles, tile_pos, tile_count, degree, cotangent):
    capacity = tiles.shape[1]
    order = jnp.arange(capacity, dtype=jnp.int32)
    hit = (tile_pos[0][None, :] == jnp.arange(64, dtype=jnp.int32)[:, None]) & (order < tile_count[0, 0])[None, :]
    slots = jnp.max(jnp.where(hit, order[None, :], -1), axis=1)
    vmem, hbm = pl.BlockSpec(memory_space=pltpu.VMEM), pl.BlockSpec(memory_space=pl.ANY)
    dma = pltpu.SemaphoreType.DMA
    hidden, grads = pl.pallas_call(
        kernel,
        out_shape=(
            jax.ShapeDtypeStruct((ND, WIDTH), BF16),
            jax.ShapeDtypeStruct((2, 4, TILE, WIDTH), BF16),
        ),
        in_specs=[vmem, hbm, hbm, hbm, pl.BlockSpec(memory_space=pltpu.SMEM), vmem, vmem],
        out_specs=(vmem, vmem),
        scratch_shapes=[
            pltpu.VMEM((capacity, TILE, TILE), BF16),
            pltpu.VMEM((WIDTH, WIDTH), BF16),
            pltpu.VMEM((WIDTH, WIDTH), BF16),
            pltpu.VMEM((16, TILE, WIDTH), BF16),
            pltpu.VMEM((WIDTH, WIDTH), BF16),
            pltpu.VMEM((4, 4, TILE, HALF), BF16),
            pltpu.VMEM((4, 4, TILE, HALF), BF16),
            pltpu.VMEM((4, 4, TILE, HALF), BF16),
            pltpu.VMEM((4, 4, TILE, HALF), BF16),
            pltpu.VMEM((4, TILE, HALF), BF16),
            pltpu.VMEM((4, TILE, HALF), BF16),
            pltpu.VMEM((4, TILE, HALF), BF16),
            pltpu.VMEM((4, TILE, HALF), BF16),
            pltpu.VMEM((4, ND, WIDTH), BF16),
            pltpu.VMEM((4, ND, WIDTH), BF16),
            pltpu.VMEM((2, ND, WIDTH), BF16),
            pltpu.VMEM((2, ND, WIDTH), BF16),
            pltpu.VMEM((2, ND, WIDTH), BF16),
            pltpu.VMEM((16, 2, ND, TILE), BF16),
            pltpu.VMEM((16, 2, ND, TILE), BF16),
            pltpu.VMEM((4, ND, TILE), F32),
            pltpu.VMEM((4, ND, TILE), F32),
            pltpu.VMEM((8, ND, TILE), BF16),
            pltpu.VMEM((TILE, TILE), BF16),
            dma((3,)),
            *[dma((8,))] * 8,
            *[dma((4,))] * 2,
            *[dma((2,))] * 2,
            *[dma((16,))] * 4,
            *[dma((4,))] * 2,
            *[dma((8,))] * 2,
            *[dma((4,))] * 2,
            *[dma((16,))] * 4,
        ],
        compiler_params=pltpu.CompilerParams(
            collective_id=0, has_side_effects=True, vmem_limit_bytes=40 * 1024 * 1024
        ),
        name="sage_layer",
    )(features, self_weight, neigh_weight, tiles[0], slots, degree[None, :], cotangent)
    grads = grads.reshape(2, WIDTH, WIDTH)
    return (hidden, grads[0].astype(F32), grads[1].astype(F32))


def solution(mesh):
    in_specs = (
        P(("row", "col"), None),
        P(),
        P(),
        P("row", "col", None, None),
        P("row", "col"),
        P("row", "col"),
        P(("row", "col")),
        P(("row", "col"), None),
    )
    out_specs = (P(("row", "col"), None), P(), P())
    return jax.shard_map(
        per_device, mesh=mesh, in_specs=in_specs, out_specs=out_specs, check_vma=False
    )
```

time: 1770 us -> 137 us (0.08)
  waiting for transfers between devices: 1650 us -> 0 us
  Pallas kernels: 0 us -> 127 us
  blocking collectives: 42.3 us -> 0 us
  loops' own time: 26.2 us -> 0 us
  matrix products: 20.2 us -> 0 us
    psum x1 -> x0, waiting for transfers between devices: 933 us -> none  [per_device(): lax.psum((local_self, local_neigh), ('row', 'col'))]
    reduce_scatter x1 -> x0, waiting for transfers between devices: 720 us -> none  [per_device(): lax.psum_scatter(partial_sums, 'col', scatter_dimension=0, tiled=True)]
    pallas_call x0 -> x1, Pallas kernels: none -> 127 us  [per_device(): pl.pallas_call(kernel, out_shape=(jax.ShapeDtypeStruct((ND, WIDTH), BF16)...]
    all_gather x1 -> x0, blocking collectives: 42.3 us -> none  [per_device(): feature_panel = lax.all_gather(features, 'row', axis=0, tiled=True)]
    another operation x1 -> x0, loops' own time: 26.2 us -> none  [add_tiles(): lax.fori_loop(0, (live_count + group_size - 1) // group_size, one_group,...]
    dot_general x12 -> x0, matrix products: 20.2 us -> none  [the longest x8 14.8 us: one_group(): product = jnp.dot(tile_value, columns, preferred_element_type=jnp.float32)]
  transfers between devices with their start and end apart: 2 -> 0, of which waited for: 2 -> 0; matrix products, arithmetic and copies ran while one was open for 0% -> 0% of each run, Pallas kernels for 0% -> 0%
where the time goes in v1:
time: 137 us
  Pallas kernels  127 us (93%)
  local copies, waits for them, and re-layouts  6.84 us (5%)
  other arithmetic  1.78 us (1%)
    pallas_call x1, Pallas kernels, per_device(): pl.pallas_call(kernel, out_shape=(jax.ShapeDtypeStruct((ND, WIDTH), BF16)...  127 us
    unnamed x15, local copies, waits for them, and re-layouts  6.74 us

profile of v1, /device:TPU:1, one launch (start us, length us, event | category | flops | bytes accessed | tf_op | source)
XLA Modules:
  0.0 136.9 jit_solution(11515062345144797748)
XLA Ops:
  1.3 0.0 copy-start.6
  1.3 0.6 copy-done.6
  1.9 0.1 select_reduce_fusion.slots_ref
  2.0 0.0 copy-start.5
  2.1 0.6 copy-done.5
  2.7 0.0 copy-start
  2.7 1.2 copy-done
  3.9 0.0 copy-start.1
  3.9 1.0 copy-done.1
  5.0 0.0 copy-start.2
  5.0 1.0 copy-done.2
  6.0 0.0 copy-start.3
  6.0 0.8 copy-done.3
  6.8 0.0 copy-start.4
  6.8 0.8 copy-done.4
  7.5 127.0 %sage_layer.1 = (bf16[32,512]{1,0:T(8,128)(2,1)S(1)}, bf16[2,4,128,512]{3,2,1,0:T(8,128)(2,1)S(1)}) custom-call(bf16[32,512]{1,0:T(8,128)(2,1)S(1)} %copy-done.3, bf16[512,512]{1,0:T(8,128)(2,1)S(1)} %copy-done.1, bf16[512,512]{1,0:T(8,128)(2,1)S(1)} %copy-done.2, bf16[32,128,128]{2,1,0:T(8,128)(2,1)S(1)} %bitcast.11, s32[64]{0:T(128)S(1)} %select_reduce_fusion.slots_ref, ...), custom_call_target="tpu_custom_call" | custom-call | tf_op jit(solution)/shard_map/sage_layer/pallas_call | solution.py:240
  134.5 0.1 fusion.1
  134.6 1.7 %bitcast_convert_fusion = (f32[512,512]{1,0:T(8,128)}, f32[512,512]{1,0:T(8,128)}) fusion(bf16[1,4,128,512]{3,2,1,0:T(8,128)(2,1)S(1)} %get-tuple-element.7, bf16[1,4,128,512]{3,2,1,0:T(8,128)(2,1)S(1)} %get-tuple-element.8), kind=kLoop, calls=%fused_computation | loop fusion | flops 524288 | bytes 3145728 | tf_op jit(solution)/shard_map/convert_element_type | solution.py:289
  136.3 0.6 copy.13
  (1 shorter events, 0.0 us)
Async XLA Ops:
  1.3 0.7 copy-start.6
  2.0 0.7 copy-start.5
  2.7 1.2 copy-start
  3.9 1.0 copy-start.1
  5.0 1.0 copy-start.2
  6.0 0.8 copy-start.3
  6.8 0.8 copy-start.4

commit v2 on v1

v2 whole, which is shorter than its diff:
```python
import jax
import jax.numpy as jnp
from jax import lax
from jax.experimental import pallas as pl
from jax.experimental.pallas import tpu as pltpu
from jax.sharding import PartitionSpec as P

MESH = pl.DeviceIdType.MESH
BF16, F32 = jnp.bfloat16, jnp.float32
WIDTH, TILE, ND = 512, 128, 32
HALF = WIDTH // 2


def flip(value, mask, bits):
    out = 0
    for k in range(bits):
        bit = lax.rem(lax.div(value, 1 << k), 2)
        out = out + (1 << k) * ((1 - bit) if (mask >> k) & 1 else bit)
    return out


def mix(value, other, bits):
    out = 0
    for k in range(bits):
        a = lax.rem(lax.div(value, 1 << k), 2)
        b = lax.rem(lax.div(other, 1 << k), 2)
        out = out + (1 << k) * (a + b - 2 * a * b)
    return out


def rows_at(index, count):
    return pl.ds(pl.multiple_of(index * count, count), count)


def kernel(
    features_hbm, self_weight_ref, neigh_weight_ref, tiles_ref, slots_hbm, degree_hbm, cotangent_hbm,
    hidden_ref, grads_ref,
    features_ref, slots_ref, degree_ref, cotangent_ref, tiles_v, self_v, neigh_v, dense, panel, part0, part1, own0, own1, in_a0, in_a1, mid0, mid1, in_b0, in_b1,
    block, own_sums, in_c, left_over, left, gated, left_in, gated_in, section, in_z, groups, final, parts,
    word, load_sem, ag_s, ag_r, agc_s, agc_r, a_s, a_r, b_s, b_r, c_s, c_r, f_s, f_r, l_s, l_r, g_s, g_r,
    z_s, z_r, zs_s, zs_r, za_s, za_r, xy_s, xy_r, xc_s, xc_r,
):
    row, col = lax.axis_index("row"), lax.axis_index("col")
    core, z_lo = lax.rem(row, 2), lax.div(row, 2)
    z = lax.div(col, 16) * 8 + z_lo
    x, y = lax.rem(lax.div(col, 4), 4), lax.rem(col, 4)
    z_in, z_group = lax.rem(z, 4), lax.div(z, 4)

    def peer(dz=0, dx=0, dy=0, dc=0):
        zp, xp, yp, cp = flip(z, dz, 5), flip(x, dx, 2), flip(y, dy, 2), flip(core, dc, 1)
        return (lax.rem(zp, 8) * 2 + cp, lax.div(zp, 8) * 16 + xp * 4 + yp)

    def send(src, dst, ssem, rsem, to):
        copy = pltpu.make_async_remote_copy(
            src_ref=src, dst_ref=dst, send_sem=ssem, recv_sem=rsem, device_id=to, device_id_type=MESH
        )
        copy.start()
        sent.append(copy)
        return copy

    sent = []
    sources = (features_hbm, slots_hbm, tiles_ref, self_weight_ref, neigh_weight_ref, degree_hbm, cotangent_hbm)
    targets = (features_ref, slots_ref, tiles_v, self_v, neigh_v, degree_ref, cotangent_ref)
    loads = [
        pltpu.make_async_copy(source, target, load_sem.at[k])
        for k, (source, target) in enumerate(zip(sources, targets))
    ]
    for load in loads:
        load.start()

    partner = peer(dc=1)
    plane = [(m // 4, m % 4) for m in range(1, 16)]
    peers = [partner]
    peers += [peer(dz=m) for m in range(1, 8)]
    peers += [peer(dz=m) for m in (8, 24)]
    peers += [peer(dx=dx, dy=dy) for dx, dy in plane]
    barrier = pltpu.get_barrier_semaphore()
    for device in peers:
        pl.semaphore_signal(barrier, inc=1, device_id=device, device_id_type=MESH)

    loads[0].wait()
    for h in range(2):
        panel[h, rows_at(row, ND), :] = features_ref[:, h * HALF : (h + 1) * HALF]

    pl.semaphore_wait(barrier, len(peers))
    for m in (4, 8, 24):
        pl.semaphore_signal(word.at[0], inc=1, device_id=peer(dz=m), device_id_type=MESH)

    mine = rows_at(row, ND)
    halves = [features_ref.at[:, h * HALF : (h + 1) * HALF] for h in range(2)]
    gather = [
        {
            m: send(halves[h], panel.at[h, mine, :], ag_s.at[h, m], ag_r.at[h, m], peer(dz=m)) for m in (4, 2, 1)
        }
        for h in range(2)
    ]
    across = [
        [send(halves[h], panel.at[h, mine, :], agc_s.at[h, 0], agc_r.at[h, 0], partner)] for h in range(2)
    ]

    for load in loads[1:3]:
        load.wait()

    def place(t, carry):
        dz = mix(lax.div(t, 4), lax.div(col, 16), 2)
        dx = mix(lax.rem(t, 4), x, 2)
        for q in range(4):
            slot = slots_ref[t * 4 + q]
            tile = tiles_v[jnp.maximum(slot, 0)]
            tile = jnp.where(slot >= 0, tile, jnp.zeros_like(tile))
            for yc in range(4):
                dy = mix(jnp.int32(yc), y, 2)
                dense[dx * 4 + dy, rows_at(dz, ND), q * TILE : (q + 1) * TILE] = tile[yc * ND : (yc + 1) * ND]
        return carry

    lax.fori_loop(0, 16, place, 0)

    def arrived(h, m, passed_on):
        gather[h][m].wait_recv()
        theirs = panel.at[h, rows_at(flip(z_lo, m, 3) * 2 + core, ND), :]
        for step in passed_on:
            origin = m + step
            gather[h][origin] = send(theirs, theirs, ag_s.at[h, origin], ag_r.at[h, origin], peer(dz=step))
        across[h].append(send(theirs, theirs, agc_s.at[h, m], agc_r.at[h, m], partner))

    for h in range(2):
        arrived(h, 4, (2, 1))
        arrived(h, 2, (1,))
        arrived(h, 6, (1,))
    loads[3].wait()

    along_x, along_y = [], []
    for h in range(2):
        for m in (1, 3, 5, 7):
            arrived(h, m, ())
        for copy in across[h]:
            copy.wait_recv()
        first, second = {}, {}
        for dx in (2, 1, 3, 0):
            lhs = dense[dx * 4 : dx * 4 + 4].reshape(4 * TILE, WIDTH)
            product = jnp.dot(lhs, panel[h], preferred_element_type=F32)
            for dy in range(4):
                rows = product[dy * TILE : (dy + 1) * TILE]
                if dx:
                    part0[h, dx, dy] = rows[:, :TILE].astype(BF16)
                else:
                    own0[h, dy] = rows[:, :TILE]
                if dy:
                    part1[h, dy, dx] = rows[:, TILE:].astype(BF16)
                else:
                    own1[h, dx] = rows[:, TILE:]
            if dx:
                first[dx] = send(part0.at[h, dx], in_a0.at[h, dx], a_s.at[h, dx], a_r.at[h, dx], peer(dx=dx))
        for dy in (2, 1, 3):
            second[dy] = send(part1.at[h, dy], in_a1.at[h, dy], a_s.at[h, 4 + dy], a_r.at[h, 4 + dy], peer(dy=dy))
        along_x.append(first)
        along_y.append(second)

    def total(own, parts):
        out = own.astype(F32)
        for value in parts:
            out = out + value.astype(F32)
        return out

    far = []
    for h in range(2):
        first, second = {}, {}
        for copy in along_x[h].values():
            copy.wait_recv()
        for k in (2, 1, 3, 0):
            value = total(own0[h, k], [in_a0[h, m, k] for m in (1, 2, 3)])
            if k:
                mid0[h, k] = value.astype(BF16)
                first[k] = send(mid0.at[h, k], in_b0.at[h, k], b_s.at[h, k], b_r.at[h, k], peer(dy=k))
            else:
                own0[h, 0] = value
        for copy in along_y[h].values():
            copy.wait_recv()
        for k in (2, 1, 3, 0):
            value = total(own1[h, k], [in_a1[h, m, k] for m in (1, 2, 3)])
            if k:
                mid1[h, k] = value.astype(BF16)
                second[k] = send(mid1.at[h, k], in_b1.at[h, k], b_s.at[h, 4 + k], b_r.at[h, 4 + k], peer(dx=k))
            else:
                own1[h, 0] = value
        for copy in first.values():
            copy.wait_recv()
        if h == 0:
            pl.semaphore_wait(word.at[0], 3)
            pl.semaphore_signal(word.at[1], inc=1, device_id=peer(dz=4), device_id_type=MESH)
        low = total(own0[h, 0], [in_b0[h, m] for m in (1, 2, 3)])
        for copy in second.values():
            copy.wait_recv()
        high = total(own1[h, 0], [in_b1[h, m] for m in (1, 2, 3)])
        for k in (2, 1, 3):
            block[h, k, :, :TILE] = low[k * ND : (k + 1) * ND].astype(BF16)
            block[h, k, :, TILE:] = high[k * ND : (k + 1) * ND].astype(BF16)
            far.append(send(block.at[h, k], in_c.at[h, k], c_s.at[h, k], c_r.at[h, k], peer(dz=8 * k)))
        own_sums[:, h * HALF : h * HALF + TILE] = low[:ND]
        own_sums[:, h * HALF + TILE : (h + 1) * HALF] = high[:ND]

    def spread_left():
        for dx, dy in plane:
            m = dx * 4 + dy
            lanes = rows_at(flip(x, dx, 2), TILE)
            left_copy(m, lanes, peer(dx=dx, dy=dy)).start()
        left_in[0] = left[:, :, rows_at(x, TILE)]

    def left_copy(m, lanes, to):
        return pltpu.make_async_remote_copy(
            src_ref=left.at[:, :, lanes], dst_ref=left_in.at[m], send_sem=l_s.at[m], recv_sem=l_r.at[m],
            device_id=to, device_id_type=MESH,
        )

    @pl.when(core == 0)
    def _():
        left[0] = features_ref[...]
        for h in range(2):
            left[1, :, h * HALF : (h + 1) * HALF] = panel[h, rows_at(row + 1, ND), :]
        spread_left()

    own_part = jnp.dot(features_ref[...], self_v[...], preferred_element_type=F32)
    for load in loads[4:]:
        load.wait()
    degree = jnp.broadcast_to(degree_ref[...].astype(F32), (ND, ND))
    eye = lax.broadcasted_iota(jnp.int32, (ND, ND), 0) == lax.broadcasted_iota(jnp.int32, (ND, ND), 1)
    scale = lax.rsqrt(jnp.sum(jnp.where(eye, degree, 0.0), axis=1, keepdims=True))
    for copy in far:
        copy.wait_recv()
    for h in range(2):
        lanes = slice(h * HALF, (h + 1) * HALF)
        own_sums[:, lanes] = total(own_sums[:, lanes], [in_c[h, k] for k in (1, 2, 3)])
    sums = own_sums[...]

    aggregated = (sums * scale).astype(BF16)
    before = own_part + jnp.dot(aggregated, neigh_v[...], preferred_element_type=F32)
    sigma = 1.0 / (1.0 + jnp.exp(-before))
    gate = (cotangent_ref[...].astype(F32) * sigma * (1.0 + before * (1.0 - sigma))).astype(BF16)
    hidden_ref[...] = (before * sigma).astype(BF16)
    gated[0] = gate
    pair = send(gated.at[0], gated.at[1], f_s.at[0], f_r.at[0], partner)
    hand_over = pltpu.make_async_remote_copy(
        src_ref=left_over, dst_ref=left.at[1], send_sem=f_s.at[1], recv_sem=f_r.at[1],
        device_id=partner, device_id_type=MESH,
    )

    @pl.when(core == 0)
    def _():
        left_over[...] = aggregated
        hand_over.start()

    @pl.when(core == 1)
    def _():
        left[0] = aggregated

    pair.wait_recv()
    swaps = []
    for dx, dy in plane:
        m = dx * 4 + dy
        lanes_y = rows_at(flip(y, dy, 2), TILE)
        swaps.append(send(gated.at[:, :, lanes_y], gated_in.at[m], g_s.at[m], g_r.at[m], peer(dx=dx, dy=dy)))

    @pl.when(core == 1)
    def _():
        hand_over.wait_recv()
        spread_left()

    gated_in[0] = gated[:, :, rows_at(y, TILE)]
    for copy in swaps:
        copy.wait_recv()
    lefts = [left_copy(dx * 4 + dy, rows_at(x, TILE), peer(dx=dx, dy=dy)) for dx, dy in plane]
    for copy in lefts:
        copy.wait_recv()
    section[...] = lax.dot_general(
        left_in[...].reshape(16 * 2 * ND, TILE),
        gated_in[...].reshape(16 * 2 * ND, TILE),
        (((0,), (0,)), ((), ())),
        preferred_element_type=F32,
    ).reshape(4, ND, TILE)

    near = [
        send(section.at[flip(z_in, m, 2)], in_z.at[m], z_s.at[m], z_r.at[m], peer(dz=m)) for m in (2, 1, 3)
    ]
    for copy in near:
        copy.wait_recv()
    groups[z_group] = (section[z_in] + in_z[1] + in_z[2] + in_z[3]).astype(BF16)
    pl.semaphore_wait(word.at[1], 1)
    spread = [
        send(groups.at[z_group], groups.at[z_group], zs_s.at[m], zs_r.at[m], peer(dz=4 * m))
        for m in (4, 3, 5, 2, 6, 1, 7)
    ]
    for copy in spread:
        copy.wait_recv()
    final[0] = total(groups[0], [groups[k] for k in range(1, 8)]).astype(BF16)
    back = [send(final.at[0], final.at[m], za_s.at[m], za_r.at[m], peer(dz=m)) for m in (2, 1, 3)]

    to_plane = [peer(dx=dx, dy=dy) for dx, dy in plane]
    out = [
        send(final.at[0], parts.at[core, x, y, 0], xy_s.at[0, m], xy_r.at[0, m], to)
        for m, to in enumerate(to_plane)
    ]
    for copy in back:
        copy.wait_recv()
    rest = parts.at[core, x, y, 1:4]
    more = [send(final.at[1:4], rest, xy_s.at[1, m], xy_r.at[1, m], to) for m, to in enumerate(to_plane)]
    last = [send(final, parts.at[core, x, y], xc_s.at[0], xc_r.at[0], partner)]

    def put(c, xb, yb, pieces):
        for m in range(4):
            grads_ref[rows_at(c * 16 + xb * 4 + flip(z_in, m, 2), ND), rows_at(yb, TILE)] = pieces[m]

    put(core, x, y, final[...])
    for m, (dx, dy) in enumerate(plane):
        out[m].wait_recv()
        more[m].wait_recv()
        xb, yb = flip(x, dx, 2), flip(y, dy, 2)
        theirs = parts.at[core, xb, yb]
        last.append(send(theirs, theirs, xc_s.at[dx * 4 + dy], xc_r.at[dx * 4 + dy], partner))
        put(core, xb, yb, parts[core, xb, yb])
    for (dx, dy), copy in zip([(0, 0)] + plane, last):
        copy.wait_recv()
        xb, yb = flip(x, dx, 2), flip(y, dy, 2)
        put(1 - core, xb, yb, parts[1 - core, xb, yb])
    for copy in lefts:
        copy.wait_send()

    @pl.when(core == 0)
    def _():
        hand_over.wait_send()

    for copy in sent:
        copy.wait_send()


def per_device(features, self_weight, neigh_weight, tiles, tile_pos, tile_count, degree, cotangent):
    capacity = tiles.shape[1]
    order = jnp.arange(capacity, dtype=jnp.int32)
    hit = (tile_pos[0][None, :] == jnp.arange(64, dtype=jnp.int32)[:, None]) & (order < tile_count[0, 0])[None, :]
    slots = jnp.max(jnp.where(hit, order[None, :], -1), axis=1)
    vmem, hbm = pl.BlockSpec(memory_space=pltpu.VMEM), pl.BlockSpec(memory_space=pltpu.HBM)
    dma = pltpu.SemaphoreType.DMA
    hidden, grads = pl.pallas_call(
        kernel,
        out_shape=(
            jax.ShapeDtypeStruct((ND, WIDTH), BF16),
            jax.ShapeDtypeStruct((2 * WIDTH, WIDTH), BF16),
        ),
        in_specs=[hbm] * 7,
        out_specs=(vmem, vmem),
        scratch_shapes=[
            pltpu.VMEM((ND, WIDTH), BF16),
            pltpu.SMEM((64,), jnp.int32),
            pltpu.VMEM((1, ND), jnp.int32),
            pltpu.VMEM((ND, WIDTH), BF16),
            pltpu.VMEM((capacity, TILE, TILE), BF16),
            pltpu.VMEM((WIDTH, WIDTH), BF16),
            pltpu.VMEM((WIDTH, WIDTH), BF16),
            pltpu.VMEM((16, TILE, WIDTH), BF16),
            pltpu.VMEM((2, WIDTH, HALF), BF16),
            pltpu.VMEM((2, 4, 4, TILE, TILE), BF16),
            pltpu.VMEM((2, 4, 4, TILE, TILE), BF16),
            pltpu.VMEM((2, 4, TILE, TILE), F32),
            pltpu.VMEM((2, 4, TILE, TILE), F32),
            pltpu.VMEM((2, 4, 4, TILE, TILE), BF16),
            pltpu.VMEM((2, 4, 4, TILE, TILE), BF16),
            pltpu.VMEM((2, 4, TILE, TILE), BF16),
            pltpu.VMEM((2, 4, TILE, TILE), BF16),
            pltpu.VMEM((2, 4, TILE, TILE), BF16),
            pltpu.VMEM((2, 4, TILE, TILE), BF16),
            pltpu.VMEM((2, 4, ND, HALF), BF16),
            pltpu.VMEM((ND, WIDTH), F32),
            pltpu.VMEM((2, 4, ND, HALF), BF16),
            pltpu.VMEM((ND, WIDTH), BF16),
            pltpu.VMEM((2, ND, WIDTH), BF16),
            pltpu.VMEM((2, ND, WIDTH), BF16),
            pltpu.VMEM((16, 2, ND, TILE), BF16),
            pltpu.VMEM((16, 2, ND, TILE), BF16),
            pltpu.VMEM((4, ND, TILE), F32),
            pltpu.VMEM((4, ND, TILE), F32),
            pltpu.VMEM((8, ND, TILE), BF16),
            pltpu.VMEM((4, ND, TILE), BF16),
            pltpu.VMEM((2, 4, 4, 4, ND, TILE), BF16),
            pltpu.SemaphoreType.REGULAR((2,)),
            dma((7,)),
            *[dma((2, 8))] * 8,
            *[dma((2, 4))] * 2,
            *[dma((2,))] * 2,
            *[dma((16,))] * 4,
            *[dma((4,))] * 2,
            *[dma((8,))] * 2,
            *[dma((4,))] * 2,
            *[dma((2, 16))] * 2,
            *[dma((16,))] * 2,
        ],
        compiler_params=pltpu.CompilerParams(
            collective_id=0, has_side_effects=True, vmem_limit_bytes=60 * 1024 * 1024
        ),
        name="sage_layer",
    )(features, self_weight, neigh_weight, tiles[0], slots, degree[None, :], cotangent)
    return (hidden, grads[:WIDTH].astype(F32), grads[WIDTH:].astype(F32))


def solution(mesh):
    in_specs = (
        P(("row", "col"), None),
        P(),
        P(),
        P("row", "col", None, None),
        P("row", "col"),
        P("row", "col"),
        P(("row", "col")),
        P(("row", "col"), None),
    )
    out_specs = (P(("row", "col"), None), P(), P())
    return jax.shard_map(
        per_device, mesh=mesh, in_specs=in_specs, out_specs=out_specs, check_vma=False
    )
```

time: 137 us -> 122 us (0.89)
  Pallas kernels: 127 us -> 116 us
  local copies, waits for them, and re-layouts: 6.84 us -> 1.27 us
  other arithmetic: 1.78 us -> 3.42 us
    pallas_call x1, Pallas kernels: 127 us -> 116 us  [per_device(): pl.pallas_call(kernel, out_shape=(jax.ShapeDtypeStruct((ND, WIDTH), BF16)...]
    unnamed x15 -> x5, local copies, waits for them, and re-layouts: 6.74 us -> 1.27 us
where the time goes in v2:
time: 122 us
  Pallas kernels  116 us (95%)
  other arithmetic  3.42 us (3%)
  between operations  1.31 us (1%)
  local copies, waits for them, and re-layouts  1.27 us (1%)
    pallas_call x1, Pallas kernels, per_device(): pl.pallas_call(kernel, out_shape=(jax.ShapeDtypeStruct((ND, WIDTH), BF16)...  116 us
    convert_element_type x1, other arithmetic, per_device(): return (hidden, grads[:WIDTH].astype(F32), grads[WIDTH:].astype(F32))  2.81 us

profile of v2, /device:TPU:1, one launch (start us, length us, event | category | flops | bytes accessed | tf_op | source)
XLA Modules:
  0.0 121.9 jit_solution(9889930668032164380)
XLA Ops:
  1.3 0.0 copy-start.1
  1.3 0.6 copy-done.1
  1.9 0.6 select_reduce_fusion.slots_hbm
  2.6 115.9 %sage_layer.1 = (bf16[32,512]{1,0:T(8,128)(2,1)}, bf16[1024,512]{1,0:T(8,128)(2,1)}) custom-call(bf16[32,512]{1,0:T(8,128)(2,1)} %features_hbm.1, bf16[512,512]{1,0:T(8,128)(2,1)} %self_weight_ref.1, bf16[512,512]{1,0:T(8,128)(2,1)} %neigh_weight_ref.1, bf16[32,128,128]{2,1,0:T(8,128)(2,1)} %bitcast.5, s32[64]{0:T(128)} %select_reduce_fusion.slots_hbm, ...), custom_call_target="tpu_custom_call" | custom-call | tf_op jit(solution)/shard_map/sage_layer/pallas_call | solution.py:342
  118.5 0.0 copy-start
  118.5 2.8 %slice_convert_fusion = (f32[512,512]{1,0:T(8,128)}, f32[512,512]{1,0:T(8,128)}) fusion(bf16[1024,512]{1,0:T(8,128)(2,1)} %get-tuple-element.6), kind=kLoop, calls=%fused_computation | loop fusion | flops 524288 | bytes 3145728 | tf_op jit(solution)/shard_map/convert_element_type | solution.py:400
  121.3 0.0 copy-done
  121.3 0.6 copy.13
  (1 shorter events, 0.0 us)
Async XLA Ops:
  1.3 0.7 copy-start.1
  118.5 2.8 %copy-start = (bf16[32,512]{1,0:T(8,128)(2,1)S(1)}, bf16[32,512]{1,0:T(8,128)(2,1)}, u32[]{:S(2)}) copy-start(bf16[32,512]{1,0:T(8,128)(2,1)} %get-tuple-element.12) | copy-start | bytes 98308

commit v3 on v2

--- a/solution.py
+++ b/solution.py
@@ -33,11 +33,11 @@
 
 
 def kernel(
-    features_hbm, self_weight_ref, neigh_weight_ref, tiles_ref, slots_hbm, degree_hbm, cotangent_hbm,
+    features_hbm, self_weight_ref, neigh_weight_ref, tiles_ref, position_hbm, count_hbm, degree_hbm, cotangent_hbm,
     hidden_ref, grads_ref,
-    features_ref, slots_ref, degree_ref, cotangent_ref, tiles_v, self_v, neigh_v, dense, panel, part0, part1, own0, own1, in_a0, in_a1, mid0, mid1, in_b0, in_b1,
-    block, own_sums, in_c, left_over, left, gated, left_in, gated_in, section, in_z, groups, final, parts,
-    word, load_sem, ag_s, ag_r, agc_s, agc_r, a_s, a_r, b_s, b_r, c_s, c_r, f_s, f_r, l_s, l_r, g_s, g_r,
+    features_ref, position_ref, count_ref, slots_v, slots_ref, degree_ref, cotangent_ref, tiles_v, self_v, neigh_v, dense, panel, part0, part1, own0, own1, in_a0, in_a1, mid0, mid1, in_b0, in_b1,
+    block, own_sums, in_c, ours, left, gated, left_in, gated_in, section, in_z, groups, final, parts,
+    word, load_sem, ag_s, ag_r, agc_s, agc_r, a_s, a_r, b_s, b_r, c_s, c_r, e_s, e_r, l_s, l_r, g_s, g_r,
     z_s, z_r, zs_s, zs_r, za_s, za_r, xy_s, xy_r, xc_s, xc_r,
 ):
     row, col = lax.axis_index("row"), lax.axis_index("col")
@@ -59,8 +59,8 @@
         return copy
 
     sent = []
-    sources = (features_hbm, slots_hbm, tiles_ref, self_weight_ref, neigh_weight_ref, degree_hbm, cotangent_hbm)
-    targets = (features_ref, slots_ref, tiles_v, self_v, neigh_v, degree_ref, cotangent_ref)
+    sources = (features_hbm, position_hbm, count_hbm, tiles_ref, self_weight_ref, neigh_weight_ref, degree_hbm, cotangent_hbm)
+    targets = (features_ref, position_ref, count_ref, tiles_v, self_v, neigh_v, degree_ref, cotangent_ref)
     loads = [
         pltpu.make_async_copy(source, target, load_sem.at[k])
         for k, (source, target) in enumerate(zip(sources, targets))
@@ -73,7 +73,7 @@
     peers = [partner]
     peers += [peer(dz=m) for m in range(1, 8)]
     peers += [peer(dz=m) for m in (8, 24)]
-    peers += [peer(dx=dx, dy=dy) for dx, dy in plane]
+    peers += [peer(dx=dx, dy=dy, dc=dc) for dx, dy in plane for dc in range(2)]
     barrier = pltpu.get_barrier_semaphore()
     for device in peers:
         pl.semaphore_signal(barrier, inc=1, device_id=device, device_id_type=MESH)
@@ -90,7 +90,7 @@
     halves = [features_ref.at[:, h * HALF : (h + 1) * HALF] for h in range(2)]
     gather = [
         {
-            m: send(halves[h], panel.at[h, mine, :], ag_s.at[h, m], ag_r.at[h, m], peer(dz=m)) for m in (4, 2, 1)
+            m: send(halves[h], panel.at[h, mine, :], ag_s.at[h, m], ag_r.at[h, m], peer(dz=m)) for m in (4, 3, 2, 1)
         }
         for h in range(2)
     ]
@@ -98,14 +98,23 @@
         [send(halves[h], panel.at[h, mine, :], agc_s.at[h, 0], agc_r.at[h, 0], partner)] for h in range(2)
     ]
 
-    for load in loads[1:3]:
+    for load in loads[1:4]:
         load.wait()
+    at = lax.broadcasted_iota(jnp.int32, (64, 32), 0)
+    order = lax.broadcasted_iota(jnp.int32, (64, 32), 1)
+    hit = jnp.broadcast_to(position_ref[...], (64, 32)) == at
+    live = order < count_ref[0, 0]
+    found = jnp.sum(jnp.where(hit & live, order + 1, 0), axis=1, keepdims=True) - 1
+    slots_v[...] = jnp.broadcast_to(found, (64, TILE))
+    to_scalars = pltpu.make_async_copy(slots_v, slots_ref, load_sem.at[8])
+    to_scalars.start()
+    to_scalars.wait()
 
     def place(t, carry):
         dz = mix(lax.div(t, 4), lax.div(col, 16), 2)
         dx = mix(lax.rem(t, 4), x, 2)
         for q in range(4):
-            slot = slots_ref[t * 4 + q]
+            slot = slots_ref[t * 4 + q, 0]
             tile = tiles_v[jnp.maximum(slot, 0)]
             tile = jnp.where(slot >= 0, tile, jnp.zeros_like(tile))
             for yc in range(4):
@@ -124,14 +133,12 @@
         across[h].append(send(theirs, theirs, agc_s.at[h, m], agc_r.at[h, m], partner))
 
     for h in range(2):
-        arrived(h, 4, (2, 1))
-        arrived(h, 2, (1,))
-        arrived(h, 6, (1,))
-    loads[3].wait()
+        arrived(h, 4, (3, 2, 1))
+    loads[4].wait()
 
     along_x, along_y = [], []
     for h in range(2):
-        for m in (1, 3, 5, 7):
+        for m in (1, 2, 3, 5, 6, 7):
             arrived(h, m, ())
         for copy in across[h]:
             copy.wait_recv()
@@ -199,17 +206,10 @@
         own_sums[:, h * HALF : h * HALF + TILE] = low[:ND]
         own_sums[:, h * HALF + TILE : (h + 1) * HALF] = high[:ND]
 
-    def spread_left():
-        for dx, dy in plane:
-            m = dx * 4 + dy
-            lanes = rows_at(flip(x, dx, 2), TILE)
-            left_copy(m, lanes, peer(dx=dx, dy=dy)).start()
-        left_in[0] = left[:, :, rows_at(x, TILE)]
-
-    def left_copy(m, lanes, to):
+    def early_copy(m, dx, dy):
         return pltpu.make_async_remote_copy(
-            src_ref=left.at[:, :, lanes], dst_ref=left_in.at[m], send_sem=l_s.at[m], recv_sem=l_r.at[m],
-            device_id=to, device_id_type=MESH,
+            src_ref=left.at[:, :, rows_at(flip(x, dx, 2), TILE)], dst_ref=left_in.at[m],
+            send_sem=e_s.at[m], recv_sem=e_r.at[m], device_id=peer(dx=dx, dy=dy), device_id_type=MESH,
         )
 
     @pl.when(core == 0)
@@ -217,10 +217,12 @@
         left[0] = features_ref[...]
         for h in range(2):
             left[1, :, h * HALF : (h + 1) * HALF] = panel[h, rows_at(row + 1, ND), :]
-        spread_left()
+        for m, (dx, dy) in enumerate(plane):
+            early_copy(m + 1, dx, dy).start()
+        left_in[0] = left[:, :, rows_at(x, TILE)]
 
     own_part = jnp.dot(features_ref[...], self_v[...], preferred_element_type=F32)
-    for load in loads[4:]:
+    for load in loads[5:]:
         load.wait()
     degree = jnp.broadcast_to(degree_ref[...].astype(F32), (ND, ND))
     eye = lax.broadcasted_iota(jnp.int32, (ND, ND), 0) == lax.broadcasted_iota(jnp.int32, (ND, ND), 1)
@@ -233,43 +235,60 @@
     sums = own_sums[...]
 
     aggregated = (sums * scale).astype(BF16)
+    ours[...] = aggregated
+
+    def left_copy(m, dx, dy, source_core):
+        to = (z_lo * 2 + 1, lax.div(col, 16) * 16 + flip(x, dx, 2) * 4 + flip(y, dy, 2))
+        return pltpu.make_async_remote_copy(
+            src_ref=ours.at[:, rows_at(flip(x, dx, 2), TILE)], dst_ref=left_in.at[m, source_core],
+            send_sem=l_s.at[m, source_core], recv_sem=l_r.at[m, source_core], device_id=to, device_id_type=MESH,
+        )
+
+    square = [(0, 0)] + plane
+    for m, (dx, dy) in enumerate(square):
+        if m:
+            left_copy(m, dx, dy, core).start()
+
+    @pl.when(core == 0)
+    def _():
+        left_copy(0, 0, 0, 0).start()
+
+    @pl.when(core == 1)
+    def _():
+        left_in[0, 1] = ours[:, rows_at(x, TILE)]
+
     before = own_part + jnp.dot(aggregated, neigh_v[...], preferred_element_type=F32)
     sigma = 1.0 / (1.0 + jnp.exp(-before))
     gate = (cotangent_ref[...].astype(F32) * sigma * (1.0 + before * (1.0 - sigma))).astype(BF16)
     hidden_ref[...] = (before * sigma).astype(BF16)
-    gated[0] = gate
-    pair = send(gated.at[0], gated.at[1], f_s.at[0], f_r.at[0], partner)
-    hand_over = pltpu.make_async_remote_copy(
-        src_ref=left_over, dst_ref=left.at[1], send_sem=f_s.at[1], recv_sem=f_r.at[1],
-        device_id=partner, device_id_type=MESH,
-    )
+    gated[...] = gate
+    swaps = []
+    for m, (dx, dy) in enumerate(square):
+        lanes = rows_at(flip(y, dy, 2), TILE)
+        for dc in range(2):
+            if m or dc:
+                swaps.append(
+                    send(
+                        gated.at[:, lanes], gated_in.at[m, core], g_s.at[m, dc], g_r.at[m, dc],
+                        peer(dx=dx, dy=dy, dc=dc),
+                    )
+                )
+    gated_in[0, core] = gated[:, rows_at(y, TILE)]
 
     @pl.when(core == 0)
     def _():
-        left_over[...] = aggregated
-        hand_over.start()
+        for m, (dx, dy) in enumerate(plane):
+            early_copy(m + 1, dx, dy).wait_recv()
 
     @pl.when(core == 1)
     def _():
-        left[0] = aggregated
-
-    pair.wait_recv()
-    swaps = []
-    for dx, dy in plane:
-        m = dx * 4 + dy
-        lanes_y = rows_at(flip(y, dy, 2), TILE)
-        swaps.append(send(gated.at[:, :, lanes_y], gated_in.at[m], g_s.at[m], g_r.at[m], peer(dx=dx, dy=dy)))
-
-    @pl.when(core == 1)
-    def _():
-        hand_over.wait_recv()
-        spread_left()
-
-    gated_in[0] = gated[:, :, rows_at(y, TILE)]
+        left_copy(0, 0, 0, 0).wait_recv()
+        for m, (dx, dy) in enumerate(square):
+            if m:
+                left_copy(m, dx, dy, 0).wait_recv()
+                left_copy(m, dx, dy, 1).wait_recv()
+
     for copy in swaps:
-        copy.wait_recv()
-    lefts = [left_copy(dx * 4 + dy, rows_at(x, TILE), peer(dx=dx, dy=dy)) for dx, dy in plane]
-    for copy in lefts:
         copy.wait_recv()
     section[...] = lax.dot_general(
         left_in[...].reshape(16 * 2 * ND, TILE),
@@ -295,38 +314,50 @@
     back = [send(final.at[0], final.at[m], za_s.at[m], za_r.at[m], peer(dz=m)) for m in (2, 1, 3)]
 
     to_plane = [peer(dx=dx, dy=dy) for dx, dy in plane]
-    out = [
-        send(final.at[0], parts.at[core, x, y, 0], xy_s.at[0, m], xy_r.at[0, m], to)
-        for m, to in enumerate(to_plane)
-    ]
-    for copy in back:
-        copy.wait_recv()
-    rest = parts.at[core, x, y, 1:4]
-    more = [send(final.at[1:4], rest, xy_s.at[1, m], xy_r.at[1, m], to) for m, to in enumerate(to_plane)]
-    last = [send(final, parts.at[core, x, y], xc_s.at[0], xc_r.at[0], partner)]
-
-    def put(c, xb, yb, pieces):
-        for m in range(4):
-            grads_ref[rows_at(c * 16 + xb * 4 + flip(z_in, m, 2), ND), rows_at(yb, TILE)] = pieces[m]
-
-    put(core, x, y, final[...])
-    for m, (dx, dy) in enumerate(plane):
-        out[m].wait_recv()
-        more[m].wait_recv()
-        xb, yb = flip(x, dx, 2), flip(y, dy, 2)
-        theirs = parts.at[core, xb, yb]
-        last.append(send(theirs, theirs, xc_s.at[dx * 4 + dy], xc_r.at[dx * 4 + dy], partner))
-        put(core, xb, yb, parts[core, xb, yb])
-    for (dx, dy), copy in zip([(0, 0)] + plane, last):
-        copy.wait_recv()
-        xb, yb = flip(x, dx, 2), flip(y, dy, 2)
-        put(1 - core, xb, yb, parts[1 - core, xb, yb])
-    for copy in lefts:
-        copy.wait_send()
+    pieces = (slice(0, 1), slice(1, 2), slice(2, 4))
+    out = []
+    for k, piece in enumerate(pieces):
+        for copy in ((), back[1:2], back[::2])[k]:
+            copy.wait_recv()
+        mine_there = parts.at[core, x, y, piece]
+        out.append(
+            [
+                send(final.at[piece], mine_there, xy_s.at[k, m], xy_r.at[k, m], to)
+                for m, to in enumerate(to_plane)
+            ]
+        )
+    last = [[], []]
+
+    def put(c, xb, yb, lo, value):
+        for m in range(2):
+            grads_ref[rows_at(c * 16 + xb * 4 + flip(z_in, lo + m, 2), ND), rows_at(yb, TILE)] = value[m]
+
+    for part in range(2):
+        both = slice(part * 2, part * 2 + 2)
+        theirs = parts.at[core, x, y, both]
+        last[part].append(send(final.at[both], theirs, xc_s.at[part, 0], xc_r.at[part, 0], partner))
+        put(core, x, y, part * 2, final[both])
+        for m, (dx, dy) in enumerate(plane):
+            for copies in (out[:2], out[2:])[part]:
+                copies[m].wait_recv()
+            xb, yb = flip(x, dx, 2), flip(y, dy, 2)
+            theirs = parts.at[core, xb, yb, both]
+            last[part].append(send(theirs, theirs, xc_s.at[part, m + 1], xc_r.at[part, m + 1], partner))
+            put(core, xb, yb, part * 2, parts[core, xb, yb, both])
+    for part in range(2):
+        for (dx, dy), copy in zip(square, last[part]):
+            copy.wait_recv()
+            xb, yb = flip(x, dx, 2), flip(y, dy, 2)
+            put(1 - core, xb, yb, part * 2, parts[1 - core, xb, yb, part * 2 : part * 2 + 2])
+    for m, (dx, dy) in enumerate(square):
+        if m:
+            left_copy(m, dx, dy, core).wait_send()
 
     @pl.when(core == 0)
     def _():
-        hand_over.wait_send()
+        left_copy(0, 0, 0, 0).wait_send()
+        for m, (dx, dy) in enumerate(plane):
+            early_copy(m + 1, dx, dy).wait_send()
 
     for copy in sent:
         copy.wait_send()
@@ -334,9 +365,6 @@
 
 def per_device(features, self_weight, neigh_weight, tiles, tile_pos, tile_count, degree, cotangent):
     capacity = tiles.shape[1]
-    order = jnp.arange(capacity, dtype=jnp.int32)
-    hit = (tile_pos[0][None, :] == jnp.arange(64, dtype=jnp.int32)[:, None]) & (order < tile_count[0, 0])[None, :]
-    slots = jnp.max(jnp.where(hit, order[None, :], -1), axis=1)
     vmem, hbm = pl.BlockSpec(memory_space=pltpu.VMEM), pl.BlockSpec(memory_space=pltpu.HBM)
     dma = pltpu.SemaphoreType.DMA
     hidden, grads = pl.pallas_call(
@@ -345,11 +373,14 @@
             jax.ShapeDtypeStruct((ND, WIDTH), BF16),
             jax.ShapeDtypeStruct((2 * WIDTH, WIDTH), BF16),
         ),
-        in_specs=[hbm] * 7,
+        in_specs=[hbm] * 8,
         out_specs=(vmem, vmem),
         scratch_shapes=[
             pltpu.VMEM((ND, WIDTH), BF16),
-            pltpu.SMEM((64,), jnp.int32),
+            pltpu.VMEM((1, 32), jnp.int32),
+            pltpu.SMEM((1, 1), jnp.int32),
+            pltpu.VMEM((64, TILE), jnp.int32),
+            pltpu.SMEM((64, TILE), jnp.int32),
             pltpu.VMEM((1, ND), jnp.int32),
             pltpu.VMEM((ND, WIDTH), BF16),
             pltpu.VMEM((capacity, TILE, TILE), BF16),
@@ -372,7 +403,7 @@
             pltpu.VMEM((2, 4, ND, HALF), BF16),
             pltpu.VMEM((ND, WIDTH), BF16),
             pltpu.VMEM((2, ND, WIDTH), BF16),
-            pltpu.VMEM((2, ND, WIDTH), BF16),
+            pltpu.VMEM((ND, WIDTH), BF16),
             pltpu.VMEM((16, 2, ND, TILE), BF16),
             pltpu.VMEM((16, 2, ND, TILE), BF16),
             pltpu.VMEM((4, ND, TILE), F32),
@@ -381,22 +412,22 @@
             pltpu.VMEM((4, ND, TILE), BF16),
             pltpu.VMEM((2, 4, 4, 4, ND, TILE), BF16),
             pltpu.SemaphoreType.REGULAR((2,)),
-            dma((7,)),
+            dma((9,)),
             *[dma((2, 8))] * 8,
             *[dma((2, 4))] * 2,
-            *[dma((2,))] * 2,
-            *[dma((16,))] * 4,
+            *[dma((16,))] * 2,
+            *[dma((16, 2))] * 4,
             *[dma((4,))] * 2,
             *[dma((8,))] * 2,
             *[dma((4,))] * 2,
+            *[dma((3, 16))] * 2,
             *[dma((2, 16))] * 2,
-            *[dma((16,))] * 2,
         ],
         compiler_params=pltpu.CompilerParams(
             collective_id=0, has_side_effects=True, vmem_limit_bytes=60 * 1024 * 1024
         ),
         name="sage_layer",
-    )(features, self_weight, neigh_weight, tiles[0], slots, degree[None, :], cotangent)
+    )(features, self_weight, neigh_weight, tiles[0], tile_pos, tile_count, degree[None, :], cotangent)
     return (hidden, grads[:WIDTH].astype(F32), grads[WIDTH:].astype(F32))
 
 

time: 122 us -> 118 us (0.967)
  Pallas kernels: 116 us -> 113 us
    pallas_call x1, Pallas kernels: 116 us -> 113 us  [per_device(): pl.pallas_call(kernel, out_shape=(jax.ShapeDtypeStruct((ND, WIDTH), BF16)...]
where the time goes in v3:
time: 118 us
  Pallas kernels  113 us (96%)
  other arithmetic  2.81 us (2%)
  between operations  1.3 us (1%)
    pallas_call x1, Pallas kernels, per_device(): pl.pallas_call(kernel, out_shape=(jax.ShapeDtypeStruct((ND, WIDTH), BF16)...  113 us
    convert_element_type x1, other arithmetic, per_device(): return (hidden, grads[:WIDTH].astype(F32), grads[WIDTH:].astype(F32))  2.81 us

profile of v3, /device:TPU:1, one launch (start us, length us, event | category | flops | bytes accessed | tf_op | source)
XLA Modules:
  0.0 118.2 jit_solution(12497235531071436732)
XLA Ops:
  1.3 113.4 %sage_layer.1 = (bf16[32,512]{1,0:T(8,128)(2,1)}, bf16[1024,512]{1,0:T(8,128)(2,1)}) custom-call(bf16[32,512]{1,0:T(8,128)(2,1)} %features_hbm.1, bf16[512,512]{1,0:T(8,128)(2,1)} %self_weight_ref.1, bf16[512,512]{1,0:T(8,128)(2,1)} %neigh_weight_ref.1, bf16[32,128,128]{2,1,0:T(8,128)(2,1)} %bitcast.2, s32[1,32]{1,0:T(1,128)} %position_hbm.1, ...), custom_call_target="tpu_custom_call" | custom-call | tf_op jit(solution)/shard_map/sage_layer/pallas_call | solution.py:370
  114.7 0.0 copy-start
  114.7 2.8 %slice_convert_fusion = (f32[512,512]{1,0:T(8,128)}, f32[512,512]{1,0:T(8,128)}) fusion(bf16[1024,512]{1,0:T(8,128)(2,1)} %get-tuple-element.6), kind=kLoop, calls=%fused_computation | loop fusion | flops 524288 | bytes 3145728 | tf_op jit(solution)/shard_map/convert_element_type | solution.py:431
  117.5 0.0 copy-done
  117.5 0.6 copy.13
Async XLA Ops:
  114.7 2.8 %copy-start = (bf16[32,512]{1,0:T(8,128)(2,1)S(1)}, bf16[32,512]{1,0:T(8,128)(2,1)}, u32[]{:S(2)}) copy-start(bf16[32,512]{1,0:T(8,128)(2,1)} %get-tuple-element.12) | copy-start | bytes 98308
